TPU v7x, 256 devices: a whole 4x4x8 slice. The times are simulated.
256 devices in a mesh: elec: 4 (over z_hi), cell: 32 (over y, x, z_lo), gate: 2 (over core).
Axes of the slice: x: 4, y: 4, z: 8 (z_hi: 4, z_lo: 2; z = z_hi * 2 + z_lo), core: 2. Of those that a mesh axis runs over, the one named last changes fastest.
Arguments:
- panels: bfloat16 [3, 2048, 8192], P(None, 'elec', 'cell'), may hold values from -6 to 6
- conductivity: float32 [8192], P('cell'), may hold values from 0.3 to 3
- residuals: bfloat16 [16, 16, 4, 128, 128], P('gate', 'elec', None, 'cell'), may hold values from -0.01171875 to 0.01171875
- gate_weight: float32 [16], P('gate'), may hold values from 0.3 to 2
- pattern: int32 [16, 4], P('elec'), may hold values from 0 to 15, as said below
- live_count: int32 [16], P('elec'), may hold values from 1 to 4, as said below
Outputs:
- grad: float32 [16, 8192], P('gate', 'cell')
- update: float32 [8192], P('cell')
Inputs may be any that keep to these rules, and one draw needn't show every extreme that they name: `pattern`: the entries of a row are distinct block numbers, and the first entry of row i is i itself; every block number appears. `live_count`: both ends are reached in every draw.
All inputs are finite; a program needn't handle non-finite values.
Results may differ from a plain program's by a relative error of at most 0.0003.
Values may be sent and summed in bfloat16 or wider, within the bound.
A program may use at most 64 MiB of HBM per device.

v0:
```python
import jax
import jax.numpy as jnp
from jax import lax
from jax.sharding import PartitionSpec as P


def pick_block(res_all, row_block, column):
    return lax.dynamic_index_in_dim(
        lax.dynamic_index_in_dim(res_all, row_block, 1, False), column, 1, False
    )


def pair_loop(running, term, pattern, live_count):
    list_len = pattern.shape[1]

    def visit_pair(position, total):
        row_block = position // list_len
        column = position % list_len
        target_block = pattern[row_block, column]
        return lax.cond(
            column < live_count[row_block],
            lambda current: current + term(row_block, column, target_block),
            lambda current: current,
            total,
        )

    return lax.fori_loop(0, pattern.shape[0] * list_len, visit_pair, running)


def rows_term(res_piece, start, panels, whole, block_size):
    height = res_piece.shape[3]

    def term(row_block, column, target_block):
        source = lax.dynamic_slice_in_dim(panels, row_block * block_size + start, height, 1)
        target = lax.dynamic_slice_in_dim(whole, target_block * block_size, block_size, 1)
        block = pick_block(res_piece, row_block, column)
        mixed = jnp.einsum("tab,mbc->tmac", block, target, preferred_element_type=jnp.float32)
        return jnp.einsum("tmac,mac->tc", mixed, source, preferred_element_type=jnp.float32)

    return term


def per_device(panels, conductivity, residuals, gate_weight, pattern, live_count):
    block_size = panels.shape[1] // pattern.shape[0]
    start_sum = jnp.zeros((residuals.shape[0], panels.shape[2]), jnp.float32)
    whole = lax.all_gather(panels, "elec", axis=1, tiled=True)
    full_res = lax.all_gather(residuals, "cell", axis=3, tiled=True)
    total = pair_loop(
        start_sum, rows_term(full_res, 0, panels, whole, block_size), pattern, live_count
    )
    partial_grad = -conductivity[None, :] * total
    grad = lax.psum(partial_grad, "elec")
    update = lax.psum(jnp.sum(gate_weight[:, None] * grad, axis=0), "gate")
    return (grad, update)


def solution(mesh):
    return jax.shard_map(
        per_device,
        mesh=mesh,
        in_specs=(
            P(None, "elec", "cell"),
            P("cell"),
            P("gate", "elec", None, "cell", None),
            P("gate"),
            P("elec", None),
            P("elec"),
        ),
        out_specs=(P("gate", "cell"), P("cell")),
        check_vma=False,
    )
```

profile of v0, /device:TPU:1, one launch (start us, length us, event | category | flops | bytes accessed | tf_op | source)
XLA Modules:
  0.0 415.8 jit_solution(8607741783233128318)
XLA Ops:
  7.2 1.6 copy.8
  10.3 151.1 %all-gather.5.cloned.1.call-done = bf16[8,4,4,128,128]{4,0,2,1,3:T(8,128)(2,1)} async-done(((bf16[8,4,4,4,128]{4,0,2,1,3:T(8,128)(2,1)}), bf16[8,4,4,128,128]{4,0,2,1,3:T(8,128)(2,1)}) %all-gather.5.cloned.1.call-update) | async-done | bytes 4194320 | tf_op jit(solution)/shard_map/all_gather | solution.py:47
  161.4 6.8 %copy.9 = bf16[8,4,4,128,128]{4,3,2,1,0:T(8,128)(2,1)} copy(bf16[8,4,4,128,128]{4,0,2,1,3:T(8,128)(2,1)} %all-gather.5.cloned.1.call-done) | data formatting | bytes 8388608 | tf_op jit(solution)/shard_map/while | solution.py:27
  168.2 78.1 %all-gather.3.cloned.1.call-done = bf16[3,2048,256]{2,1,0:T(8,128)(2,1)} async-done(((bf16[3,512,256]{2,1,0:T(8,128)(2,1)}), bf16[3,2048,256]{2,1,0:T(8,128)(2,1)}) %all-gather.3.cloned.1.call-update) | async-done | bytes 3145744 | tf_op jit(solution)/shard_map/all_gather | solution.py:46
  246.4 131.6 %while.18 = (s32[]{:T(128)}, f32[8,256]{1,0:T(8,128)S(1)}, s32[4]{0:T(128)}, bf16[3,512,256]{2,1,0:T(8,128)(2,1)}, s32[4,4]{1,0:T(4,128)}, /*index=5*/bf16[3,204...) while((s32[]{:T(128)}, f32[8,256]{1,0:T(8,128)S(1)}, ...), condition=%wide.region_3.4_spmd, body=%wide.region_0.3_spmd.sunk | while | flops 202997792 | bytes 8569424 | solution.py:27
  248.3 10.1 %conditional.2 = (f32[8,256]{1,0:T(8,128)S(1)}) conditional(s32[]{:T(128)} %convert_element_type.11, f32[8,256]{1,0:T(8,128)S(1)} %get-tuple-element.330, (s32[]{:T(128)}, bf16[3,512,256]{2,1,0:T(8,128)(2,1)}, s32[]{:T(128)}, s32[4,4]{1,0:T(4,128)}, s32[]{:T(128)}, /*index=5*/bf16[3,2048,256]{2,1,0:T(8,128)(2,1)}, ...), branch_computations={%region_1.1_spmd, %region_2.2_spmd} | conditional | flops 202997776 | bytes 8569060 | solution.py:20
  248.3 1.3 dynamic_slice.30
  250.2 1.7 convolution_bitcast_fusion
  251.9 1.7 bitcast_convert_fusion
  254.7 2.7 fusion
  260.3 10.1 %conditional.2 = (f32[8,256]{1,0:T(8,128)S(1)}) conditional(s32[]{:T(128)} %convert_element_type.11, f32[8,256]{1,0:T(8,128)S(1)} %get-tuple-element.330, (s32[]{:T(128)}, bf16[3,512,256]{2,1,0:T(8,128)(2,1)}, s32[]{:T(128)}, s32[4,4]{1,0:T(4,128)}, s32[]{:T(128)}, /*index=5*/bf16[3,2048,256]{2,1,0:T(8,128)(2,1)}, ...), branch_computations={%region_1.1_spmd, %region_2.2_spmd} | conditional | flops 202997776 | bytes 8569060 | solution.py:20
  262.2 1.7 convolution_bitcast_fusion
  263.9 1.7 bitcast_convert_fusion
  266.7 2.7 fusion
  272.3 10.1 %conditional.2 = (f32[8,256]{1,0:T(8,128)S(1)}) conditional(s32[]{:T(128)} %convert_element_type.11, f32[8,256]{1,0:T(8,128)S(1)} %get-tuple-element.330, (s32[]{:T(128)}, bf16[3,512,256]{2,1,0:T(8,128)(2,1)}, s32[]{:T(128)}, s32[4,4]{1,0:T(4,128)}, s32[]{:T(128)}, /*index=5*/bf16[3,2048,256]{2,1,0:T(8,128)(2,1)}, ...), branch_computations={%region_1.1_spmd, %region_2.2_spmd} | conditional | flops 202997776 | bytes 8569060 | solution.py:20
  274.2 1.7 convolution_bitcast_fusion
  275.9 1.7 bitcast_convert_fusion
  278.8 2.7 fusion
  286.2 10.1 %conditional.2 = (f32[8,256]{1,0:T(8,128)S(1)}) conditional(s32[]{:T(128)} %convert_element_type.11, f32[8,256]{1,0:T(8,128)S(1)} %get-tuple-element.330, (s32[]{:T(128)}, bf16[3,512,256]{2,1,0:T(8,128)(2,1)}, s32[]{:T(128)}, s32[4,4]{1,0:T(4,128)}, s32[]{:T(128)}, /*index=5*/bf16[3,2048,256]{2,1,0:T(8,128)(2,1)}, ...), branch_computations={%region_1.1_spmd, %region_2.2_spmd} | conditional | flops 202997776 | bytes 8569060 | solution.py:20
  288.1 1.7 convolution_bitcast_fusion
  289.8 1.7 bitcast_convert_fusion
  292.7 2.7 fusion
  298.2 10.1 %conditional.2 = (f32[8,256]{1,0:T(8,128)S(1)}) conditional(s32[]{:T(128)} %convert_element_type.11, f32[8,256]{1,0:T(8,128)S(1)} %get-tuple-element.330, (s32[]{:T(128)}, bf16[3,512,256]{2,1,0:T(8,128)(2,1)}, s32[]{:T(128)}, s32[4,4]{1,0:T(4,128)}, s32[]{:T(128)}, /*index=5*/bf16[3,2048,256]{2,1,0:T(8,128)(2,1)}, ...), branch_computations={%region_1.1_spmd, %region_2.2_spmd} | conditional | flops 202997776 | bytes 8569060 | solution.py:20
  300.1 1.7 convolution_bitcast_fusion
  301.8 1.7 bitcast_convert_fusion
  304.7 2.7 fusion
  314.1 10.1 %conditional.2 = (f32[8,256]{1,0:T(8,128)S(1)}) conditional(s32[]{:T(128)} %convert_element_type.11, f32[8,256]{1,0:T(8,128)S(1)} %get-tuple-element.330, (s32[]{:T(128)}, bf16[3,512,256]{2,1,0:T(8,128)(2,1)}, s32[]{:T(128)}, s32[4,4]{1,0:T(4,128)}, s32[]{:T(128)}, /*index=5*/bf16[3,2048,256]{2,1,0:T(8,128)(2,1)}, ...), branch_computations={%region_1.1_spmd, %region_2.2_spmd} | conditional | flops 202997776 | bytes 8569060 | solution.py:20
  316.0 1.7 convolution_bitcast_fusion
  317.7 1.7 bitcast_convert_fusion
  320.5 2.7 fusion
  331.8 10.1 %conditional.2 = (f32[8,256]{1,0:T(8,128)S(1)}) conditional(s32[]{:T(128)} %convert_element_type.11, f32[8,256]{1,0:T(8,128)S(1)} %get-tuple-element.330, (s32[]{:T(128)}, bf16[3,512,256]{2,1,0:T(8,128)(2,1)}, s32[]{:T(128)}, s32[4,4]{1,0:T(4,128)}, s32[]{:T(128)}, /*index=5*/bf16[3,2048,256]{2,1,0:T(8,128)(2,1)}, ...), branch_computations={%region_1.1_spmd, %region_2.2_spmd} | conditional | flops 202997776 | bytes 8569060 | solution.py:20
  333.8 1.7 convolution_bitcast_fusion
  335.4 1.7 bitcast_convert_fusion
  338.3 2.7 fusion
  343.8 10.1 %conditional.2 = (f32[8,256]{1,0:T(8,128)S(1)}) conditional(s32[]{:T(128)} %convert_element_type.11, f32[8,256]{1,0:T(8,128)S(1)} %get-tuple-element.330, (s32[]{:T(128)}, bf16[3,512,256]{2,1,0:T(8,128)(2,1)}, s32[]{:T(128)}, s32[4,4]{1,0:T(4,128)}, s32[]{:T(128)}, /*index=5*/bf16[3,2048,256]{2,1,0:T(8,128)(2,1)}, ...), branch_computations={%region_1.1_spmd, %region_2.2_spmd} | conditional | flops 202997776 | bytes 8569060 | solution.py:20
  345.8 1.7 convolution_bitcast_fusion
  347.4 1.7 bitcast_convert_fusion
  350.3 2.7 fusion
  355.8 10.1 %conditional.2 = (f32[8,256]{1,0:T(8,128)S(1)}) conditional(s32[]{:T(128)} %convert_element_type.11, f32[8,256]{1,0:T(8,128)S(1)} %get-tuple-element.330, (s32[]{:T(128)}, bf16[3,512,256]{2,1,0:T(8,128)(2,1)}, s32[]{:T(128)}, s32[4,4]{1,0:T(4,128)}, s32[]{:T(128)}, /*index=5*/bf16[3,2048,256]{2,1,0:T(8,128)(2,1)}, ...), branch_computations={%region_1.1_spmd, %region_2.2_spmd} | conditional | flops 202997776 | bytes 8569060 | solution.py:20
  357.8 1.7 convolution_bitcast_fusion
  359.5 1.7 bitcast_convert_fusion
  362.3 2.7 fusion
  367.8 10.1 %conditional.2 = (f32[8,256]{1,0:T(8,128)S(1)}) conditional(s32[]{:T(128)} %convert_element_type.11, f32[8,256]{1,0:T(8,128)S(1)} %get-tuple-element.330, (s32[]{:T(128)}, bf16[3,512,256]{2,1,0:T(8,128)(2,1)}, s32[]{:T(128)}, s32[4,4]{1,0:T(4,128)}, s32[]{:T(128)}, /*index=5*/bf16[3,2048,256]{2,1,0:T(8,128)(2,1)}, ...), branch_computations={%region_1.1_spmd, %region_2.2_spmd} | conditional | flops 202997776 | bytes 8569060 | solution.py:20
  369.8 1.7 convolution_bitcast_fusion
  371.5 1.7 bitcast_convert_fusion
  374.3 2.7 fusion
  378.0 25.7 %psum.14 = f32[8,256]{1,0:T(8,128)S(1)} all-reduce(f32[8,256]{1,0:T(8,128)S(1)} %broadcast_multiply_fusion), channel_id=1, replica_groups=mesh['elec'=4,'cell'=32,'gate'=2] {'elec'}, use_global_device_ids=true, to_apply=%region_4.5 | all-reduce | flops 2048 | bytes 16384 | tf_op jit(solution)/shard_map/psum | solution.py:52
  403.8 5.1 %psum.15 = f32[256]{0:T(256)} all-reduce(f32[256]{0:T(256)S(1)} %multiply_reduce_fusion), channel_id=1, replica_groups=mesh['elec'=4,'cell'=32,'gate'=2] {'gate'}, use_global_device_ids=true, to_apply=%region_6.7 | all-reduce | flops 256 | bytes 2048 | tf_op jit(solution)/shard_map/psum | solution.py:53
  (73 shorter events, 54.3 us)
Async XLA Ops:
  7.2 154.2 %all-gather.5.cloned.1.call-start = ((), (), s32[]{:S(2)}) async-start(), calls=%async_computation.1 | async-start | bytes 4325376 | tf_op jit(solution)/shard_map/all_gather | solution.py:47
  8.9 237.5 %all-gather.3.cloned.1.call-start = ((), (), s32[]{:S(2)}) async-start(), calls=%async_computation | async-start | bytes 3932160 | tf_op jit(solution)/shard_map/all_gather | solution.py:46
  246.4 157.3 %copy-start.1 = (f32[8]{0:T(128)S(1)}, f32[8]{0:T(128)}, u32[]{:S(2)}) copy-start(f32[8]{0:T(128)} %param.13) | copy-start | bytes 100
  403.7 5.2 %copy-start = (f32[8,256]{1,0:T(8,128)}, f32[8,256]{1,0:T(8,128)S(1)}, u32[]{:S(2)}) copy-start(f32[8,256]{1,0:T(8,128)S(1)} %psum.14) | copy-start | bytes 24580
Sparse Core Ops, SparseCore 0:
  9.8 151.5 all-gather.4
  163.2 83.1 all-gather.2
where the time goes:
time: 418 us; the launch traced here: 416 us
  waiting for transfers between devices  230 us (55%)
  local copies, waits for them, and re-layouts  62.4 us (15%)
  other arithmetic  44.6 us (11%)
  blocking collectives  30.8 us (7%)
  loops' own time  17.2 us (4%)
  matrix products  16.6 us (4%)
  between operations  14.1 us (3%)
    all_gather x1, waiting for transfers between devices, per_device(): full_res = lax.all_gather(residuals, 'cell', axis=3, tiled=True)  151 us
    all_gather x1, waiting for transfers between devices, per_device(): whole = lax.all_gather(panels, 'elec', axis=1, tiled=True)  78.1 us
    cond x20, other arithmetic  43.8 us
    psum x1, blocking collectives, per_device(): grad = lax.psum(partial_grad, 'elec')  25.7 us
    dynamic_slice x16, local copies, waits for them, and re-layouts, visit_pair(): live_count[row_block]  20 us
    dot_general x10, matrix products, term(): jnp.einsum('tab,mbc->tmac', block, target, preferred_element_type=jnp.flo...  16.6 us
    dynamic_slice x10, local copies, waits for them, and re-layouts, visit_pair(): target_block = pattern[row_block, column]  12.8 us
    cond x10, local copies, waits for them, and re-layouts  11.5 us
  transfers between devices with their start and end apart: 2, of which 2 were waited for; matrix products, arithmetic and copies ran while one was open for 2% of the time, Pallas kernels for 0%

commit v1 on v0

v1 whole, which is shorter than its diff:
```python
import jax
import jax.numpy as jnp
from jax import lax
from jax.experimental import pallas as pl
from jax.experimental.pallas import tpu as pltpu
from jax.sharding import PartitionSpec as P

MESH = pl.DeviceIdType.MESH
NX, NY, NZ = 4, 4, 8
D1 = (0, 1, -1, 2)

ORDER = (
    "L10", "V0", "UA+", "UA-", "UB+0", "UB-0", "S10", "L11", "L12", "VA+", "VB+0", "VA-", "VB-0",
    "S11", "L20", "UA2+", "UA2-", "UB+1", "UB-1", "L21", "VB+1", "VB-1", "S12", "L22", "UB+-1",
    "UB--1", "VB+-1", "VB--1", "L30", "VA2+", "VA2-", "L31", "UB+2", "UB-2", "L32", "VB+2", "VB-2",
    "S20",
)


def kernel(
    p_hbm, r_ref, cond_ref, gw_ref, pat_ref, live_ref,
    grad_ref, upd_ref,
    rbuf, pall0, pall1, pall2, via, psf, mix, part, gath, rows, send, recv, local,
):
    pall = (pall0, pall1, pall2)
    cell = lax.axis_index("cell")
    e = lax.axis_index("elec")
    g = lax.axis_index("gate")
    y, x, zl = cell // (NX * 2), (cell // 2) % NX, cell % 2
    z = e * 2 + zl
    sg = 1 - 2 * g

    def cell_at(dx, dy, zlow):
        return (((y + dy + NY) % NY) * NX + (x + dx + NX) % NX) * 2 + zlow

    def xy(dx, dy):
        return {"cell": cell_at(dx, dy, zl), "elec": e, "gate": g}

    def at_z(dz, core=None):
        zz = (z + dz + 2 * NZ) % NZ
        return {"cell": cell_at(0, 0, zz % 2), "elec": zz // 2, "gate": g if core is None else core}

    z_mate = at_z(1 - 2 * zl)
    core_mate = {"cell": cell, "elec": e, "gate": 1 - g}
    peers = [at_z(d) for d in (2, 4, 6)]
    cross = [at_z(d, 1 - g) for d in (0, 2, 4, 6)]

    barrier = pltpu.get_barrier_semaphore()
    greet = [xy(1, 0), xy(-1, 0), xy(0, 1), xy(0, -1), at_z(1), at_z(-1)] + peers + cross
    for device in greet:
        pl.semaphore_signal(barrier, inc=1, device_id=device, device_id_type=MESH)

    own = [
        pltpu.make_async_copy(p_hbm.at[m], pall[m].at[pl.ds(e * 4, 4)], local.at[m])
        for m in range(3)
    ]
    for copy in own:
        copy.start()

    out_row = lax.broadcasted_iota(jnp.int32, (512, 512), 0)
    in_row = lax.broadcasted_iota(jnp.int32, (512, 512), 1)
    shuffle = jnp.where((out_row % 8) * 64 + out_row // 8 == in_row, 1.0, 0.0).astype(jnp.bfloat16)
    turned = jnp.dot(shuffle, r_ref[...], preferred_element_type=jnp.float32)
    rbuf[cell] = turned.astype(jnp.bfloat16).reshape(16, 32, 128)

    pl.semaphore_wait(barrier, len(greet))

    ids = {}
    flying = []
    landing = {}

    def go(name, src, dst, device):
        n = ids.setdefault(name, len(ids))
        copy = pltpu.make_async_remote_copy(
            src_ref=src, dst_ref=dst, send_sem=send.at[n], recv_sem=recv.at[n],
            device_id=device, device_id_type=MESH,
        )
        copy.start()
        flying.append(copy)
        landing[name] = copy

    def block(name, slot, half, device):
        ref = rbuf.at[slot] if half is None else rbuf.at[slot, pl.ds(half * 8, 8)]
        go(name, ref, ref, device)

    def step(s, axis, sign):
        along_x = (axis == 0) == (s == "U")
        return xy(sign, 0) if along_x else xy(0, sign)

    def slot_of(s, d1, d2):
        if s == "U":
            return cell_at(-d1, -d2, zl)
        return cell_at(-d2, -d1, 1 - zl)

    def panel(dz):
        origin = ((z + dz + 2 * NZ) % NZ) // 2
        return pl.ds(origin * 4 + g * 2, 2)

    def seed(s):
        slot = slot_of(s, 0, 0)
        for axis, tag, tail in ((0, "A", ""), (1, "B", "0")):
            for sign, mark in ((1, "+"), (-1, "-")):
                block(s + tag + mark + tail, slot, None, step(s, axis, sign))

    def spread(s, d1):
        slot = slot_of(s, d1, 0)
        for sign, mark in ((1, "+"), (-1, "-")):
            block(f"{s}B{mark}{d1}", slot, None, step(s, 1, sign))

    def arrived(name):
        landing[name].wait_recv()

    def pass_on(name):
        if name == "V0":
            seed("V")
        elif name[0] in "UV" and name[1:3] == "A2":
            s = name[0]
            if name[3] == "-":
                spread(s, 2)
        elif name[0] in "UV" and name[1] == "A":
            s, mark = name[0], name[2]
            sign = 1 if mark == "+" else -1
            block(f"{s}A2{mark}", slot_of(s, sign, 0), 0 if sign == 1 else 1, step(s, 0, sign))
            spread(s, sign)
        elif name[0] in "UV" and name[1:3] != "B2":
            s, mark, d1 = name[0], name[2], int(name[3:])
            sign = 1 if mark == "+" else -1
            block(f"{s}B2{mark}{d1}", slot_of(s, d1, sign), 0 if sign == 1 else 1, step(s, 1, sign))
        elif name[0] in "LS":
            m = int(name[2])
            kind = name[:2]
            if kind == "L1":
                go(f"L2{m}", via.at[0, m], pall[m].at[panel(-sg)], at_z(sg))
            elif kind == "L2":
                ref = pall[m].at[panel(-2 * sg)]
                go(f"L3{m}", ref, via.at[1, m], at_z(sg))
                go(f"W2{m}", ref, ref, core_mate)
            elif kind == "L3":
                go(f"L4{m}", via.at[1, m], pall[m].at[panel(-3 * sg)], at_z(sg))
            elif kind == "L4":
                ref = pall[m].at[panel(4)]
                go(f"W4{m}", ref, ref, core_mate)
            elif kind == "S1":
                go(f"S2{m}", via.at[2, m], pall[m].at[panel(sg)], at_z(-sg))
            elif kind == "S2":
                ref = pall[m].at[panel(2 * sg)]
                go(f"WS{m}", ref, ref, core_mate)

    block("V0", cell, None, z_mate)
    seed("U")
    half = pl.ds(g * 2, 2)
    for m in range(3):
        go(f"L1{m}", p_hbm.at[m, half], via.at[0, m], at_z(sg))
        go(f"S1{m}", p_hbm.at[m, half], via.at[2, m], at_z(-sg))

    for m in range(3):
        own[m].wait()
        psf[m] = pall[m][pl.ds(e * 4, 4)].reshape(512, 256).astype(jnp.float32)

    waited = set()

    def take(name):
        arrived(name)
        waited.add(name)
        pass_on(name)

    for name in ORDER:
        take(name)
    for name in list(ids):
        if name[0] in "UV" and name not in waited:
            take(name)

    def component(m, total):
        def source(i, acc):
            count = live_ref[i]
            target = []
            for k in range(4):
                there = pall[m][pat_ref[i, k]]
                alive = jnp.minimum(jnp.maximum(count - k, 0), 1).astype(jnp.float32)
                target.append(there * jnp.full((128, 256), alive).astype(jnp.bfloat16))
            target = jnp.concatenate(target, axis=0)
            for q in range(4):
                left = jnp.concatenate(
                    [rbuf[q * 8 : q * 8 + 8, i * 4 + k].reshape(256, 128) for k in range(4)], axis=1
                )
                mix[...] = jnp.dot(left, target, preferred_element_type=jnp.float32)
                for a in range(32):
                    row = psf[m, pl.ds(i * 128 + q * 32 + a, 1), :]
                    acc = acc + mix[a * 8 : a * 8 + 8, :] * row
            return acc

        return lax.fori_loop(0, 4, source, total)

    total = jnp.zeros((8, 256), jnp.float32)
    for m in range(3):
        for kind in ("L4", "S2"):
            if f"{kind}{m}" not in waited:
                take(f"{kind}{m}")
        for kind in ("W2", "W4", "WS"):
            arrived(f"{kind}{m}")
        total = component(m, total)

    mine = total * -cond_ref[...]
    weighted = mine[0:1] * gw_ref[0]
    for t in range(1, 8):
        weighted = weighted + mine[t : t + 1] * gw_ref[t]
    part[0:8] = mine
    part[8:16] = jnp.broadcast_to(weighted, (8, 256))
    gath[e] = part[...]
    for n, device in enumerate(peers):
        go(f"G{n}", part, gath.at[e], device)
    for n, device in enumerate(cross):
        go(f"H{n}", part.at[pl.ds(8, 8)], rows.at[e], device)
    for n in range(3):
        arrived(f"G{n}")
    for n in range(4):
        arrived(f"H{n}")
    grad_ref[...] = (gath[0, 0:8] + gath[1, 0:8]) + (gath[2, 0:8] + gath[3, 0:8])
    here = (gath[0, 8:9] + gath[1, 8:9]) + (gath[2, 8:9] + gath[3, 8:9])
    there = (rows[0, 0:1] + rows[1, 0:1]) + (rows[2, 0:1] + rows[3, 0:1])
    upd_ref[...] = here + there
    for copy in flying:
        copy.wait_send()


def per_device(panels, conductivity, residuals, gate_weight, pattern, live_count):
    vmem = pl.BlockSpec(memory_space=pltpu.VMEM)
    smem = pl.BlockSpec(memory_space=pltpu.SMEM)
    copies = 96
    grad, update = pl.pallas_call(
        kernel,
        out_shape=(
            jax.ShapeDtypeStruct((8, 256), jnp.float32),
            jax.ShapeDtypeStruct((1, 256), jnp.float32),
        ),
        in_specs=[pl.BlockSpec(memory_space=pl.ANY), vmem, vmem, smem, smem, smem],
        out_specs=(vmem, vmem),
        scratch_shapes=[
            pltpu.VMEM((32, 16, 32, 128), jnp.bfloat16),
            pltpu.VMEM((16, 128, 256), jnp.bfloat16),
            pltpu.VMEM((16, 128, 256), jnp.bfloat16),
            pltpu.VMEM((16, 128, 256), jnp.bfloat16),
            pltpu.VMEM((3, 3, 2, 128, 256), jnp.bfloat16),
            pltpu.VMEM((3, 512, 256), jnp.float32),
            pltpu.VMEM((256, 256), jnp.float32),
            pltpu.VMEM((16, 256), jnp.float32),
            pltpu.VMEM((4, 16, 256), jnp.float32),
            pltpu.VMEM((4, 8, 256), jnp.float32),
            pltpu.SemaphoreType.DMA((copies,)),
            pltpu.SemaphoreType.DMA((copies,)),
            pltpu.SemaphoreType.DMA((3,)),
        ],
        compiler_params=pltpu.CompilerParams(
            collective_id=0, has_side_effects=True, vmem_limit_bytes=40 << 20
        ),
        name="adjoint",
    )(
        panels.reshape(3, 4, 128, 256),
        residuals.reshape(512, 128),
        conductivity.reshape(1, 256),
        gate_weight,
        pattern,
        live_count,
    )
    return grad, update.reshape(256)


def solution(mesh):
    return jax.shard_map(
        per_device,
        mesh=mesh,
        in_specs=(
            P(None, "elec", "cell"),
            P("cell"),
            P("gate", "elec", None, "cell", None),
            P("gate"),
            P("elec", None),
            P("elec"),
        ),
        out_specs=(P("gate", "cell"), P("cell")),
        check_vma=False,
    )
```

time: 418 us -> 61 us (0.15)
  waiting for transfers between devices: 230 us -> 0 us
  local copies, waits for them, and re-layouts: 62.4 us -> 3.88 us
  Pallas kernels: 0 us -> 56.3 us
  other arithmetic: 44.6 us -> 0 us
  blocking collectives: 30.8 us -> 0 us
  loops' own time: 17.2 us -> 0 us
  matrix products: 16.6 us -> 0 us
  between operations: 14.1 us -> 0.68 us
    all_gather x2 -> x0, waiting for transfers between devices: 229 us -> none  [the longest x1 151 us: per_device(): full_res = lax.all_gather(residuals, 'cell', axis=3, tiled=True)]
    pallas_call x0 -> x1, Pallas kernels: none -> 56.3 us  [per_device(): pl.pallas_call(kernel, out_shape=(jax.ShapeDtypeStruct((8, 256), jnp.floa...]
    cond x20 -> x0, other arithmetic: 43.8 us -> none
    dynamic_slice x26 -> x0, local copies, waits for them, and re-layouts: 32.8 us -> none  [the longest x16 20 us: visit_pair(): live_count[row_block]]
    psum x2 -> x0, blocking collectives: 30.8 us -> none  [the longest x1 25.7 us: per_device(): grad = lax.psum(partial_grad, 'elec')]
    another operation x17 -> x0, loops' own time: 17.2 us -> none  [the longest x1 10.4 us: pair_loop(): return lax.fori_loop(0, pattern.shape[0] * list_len, visit_pair, running)]
    dot_general x10 -> x0, matrix products: 16.6 us -> none  [term(): jnp.einsum('tab,mbc->tmac', block, target, preferred_element_type=jnp.flo...]
    cond x10 -> x0, local copies, waits for them, and re-layouts: 11.5 us -> none
  transfers between devices with their start and end apart: 2 -> 0, of which waited for: 2 -> 0; matrix products, arithmetic and copies ran while one was open for 2% -> 0% of each run, Pallas kernels for 0% -> 0%
where the time goes in v1:
time: 61 us; the launch traced here: 60.9 us
  Pallas kernels  56.3 us (92%)
  local copies, waits for them, and re-layouts  3.88 us (6%)
  between operations  0.68 us (1%)
    pallas_call x1, Pallas kernels, per_device(): pl.pallas_call(kernel, out_shape=(jax.ShapeDtypeStruct((8, 256), jnp.floa...  56.3 us
    unnamed x14, local copies, waits for them, and re-layouts  3.88 us

profile of v1, /device:TPU:1, one launch (start us, length us, event | category | flops | bytes accessed | tf_op | source)
XLA Modules:
  0.0 60.9 jit_solution(7703771470829323532)
XLA Ops:
  0.6 0.0 copy-start.5
  0.6 0.0 copy-start.2
  0.7 0.0 copy-start.3
  0.7 0.0 copy-start.4
  0.7 0.6 %copy-done.5 = s32[4]{0:T(128)S(1)} copy-done((s32[4]{0:T(128)S(1)}, s32[4]{0:T(128)}, u32[]{:S(2)}) %copy-start.5) | copy-done | bytes 40
  1.3 0.0 copy-done.2
  1.3 0.0 copy-done.3
  1.3 0.0 copy-done.4
  1.3 0.0 copy-start
  1.3 1.1 %copy-done = bf16[3,512,256]{2,1,0:T(8,128)(2,1)S(1)} copy-done((bf16[3,512,256]{2,1,0:T(8,128)(2,1)S(1)}, bf16[3,512,256]{2,1,0:T(8,128)(2,1)}, u32[]{:S(2)}) %copy-start) | copy-done | bytes 786456
  2.5 0.0 copy-start.1
  2.5 0.9 %copy-done.1 = bf16[8,4,4,4,128]{4,3,2,1,0:T(4,128)(2,1)S(1)} copy-done((bf16[8,4,4,4,128]{4,3,2,1,0:T(4,128)(2,1)S(1)}, bf16[8,4,4,4,128]{4,3,2,1,0:T(4,128)(2,1)}, u32[]{:S(2)}) %copy-start.1) | copy-done | bytes 131096
  3.4 56.3 %adjoint.1 = (f32[8,256]{1,0:T(8,128)S(1)}, f32[1,256]{1,0:T(1,128)S(1)}) custom-call(bf16[3,4,128,256]{3,2,1,0:T(8,128)(2,1)S(1)} %bitcast.4, bf16[512,128]{1,0:T(8,128)(2,1)S(1)} %bitcast.5, f32[1,256]{1,0:T(1,128)S(1)} %bitcast.6, f32[8]{0:T(128)S(1)} %copy-done.4, s32[4,4]{1,0:T(4,128)S(1)} %copy-done.2, s32[4]{0:T(128)S(1)} %copy-done.5), custom_call_target="tpu_custom_call" | custom-call | tf_op jit(solution)/shard_map/adjoint/pallas_call | solution.py:230
  59.7 0.6 copy.10
  60.3 0.6 copy.11
Async XLA Ops:
  0.6 0.7 %copy-start.5 = (s32[4]{0:T(128)S(1)}, s32[4]{0:T(128)}, u32[]{:S(2)}) copy-start(s32[4]{0:T(128)} %live_ref.1) | copy-start | bytes 52
  0.6 0.7 %copy-start.2 = (s32[4,4]{1,0:T(4,128)S(1)}, s32[4,4]{1,0:T(4,128)}, u32[]{:S(2)}) copy-start(s32[4,4]{1,0:T(4,128)} %pat_ref.1) | copy-start | bytes 196
  0.7 0.7 %copy-start.3 = (f32[256]{0:T(256)S(1)}, f32[256]{0:T(256)}, u32[]{:S(2)}) copy-start(f32[256]{0:T(256)} %param.7) | copy-start | bytes 3076
  0.7 0.7 %copy-start.4 = (f32[8]{0:T(128)S(1)}, f32[8]{0:T(128)}, u32[]{:S(2)}) copy-start(f32[8]{0:T(128)} %gw_ref.1) | copy-start | bytes 100
  1.3 1.1 %copy-start = (bf16[3,512,256]{2,1,0:T(8,128)(2,1)S(1)}, bf16[3,512,256]{2,1,0:T(8,128)(2,1)}, u32[]{:S(2)}) copy-start(bf16[3,512,256]{2,1,0:T(8,128)(2,1)} %param.6) | copy-start | bytes 2359300
  2.5 0.9 %copy-start.1 = (bf16[8,4,4,4,128]{4,3,2,1,0:T(4,128)(2,1)S(1)}, bf16[8,4,4,4,128]{4,3,2,1,0:T(4,128)(2,1)}, u32[]{:S(2)}) copy-start(bf16[8,4,4,4,128]{4,3,2,1,0:T(4,128)(2,1)} %param.8) | copy-start | bytes 393220

commit v2 on v1

v2 whole, which is shorter than its diff:
```python
import jax
import jax.numpy as jnp
from jax import lax
from jax.experimental import pallas as pl
from jax.experimental.pallas import tpu as pltpu
from jax.sharding import PartitionSpec as P

MESH = pl.DeviceIdType.MESH
NX, NY, NZ = 4, 4, 8

NAMES = ["V0"]
for s in "UV":
    for way in "+-":
        NAMES += [s + "A" + way, s + "A2" + way]
        for gone in (0, 1, -1, 2):
            NAMES += [s + "B" + way + str(gone), s + "B2" + way + str(gone)]
for m in "012":
    for way in "ab":
        NAMES += [kind + m + way for kind in ("L1", "L2", "L3", "L4", "S1", "S2", "W2", "W4", "WS")]

PLAN = (
    0, 1, 11, 3, 13, 41, 50, 59, 68, 200, 77, 86, 100, 21, 31, 23, 33, 45, 54, 141, 150, 101, 111,
    103, 113, 5, 15, 2, 12, 42, 51, 159, 168, 60, 69, 177, 186, 7, 17, 78, 87, 121, 25, 35, 131,
    123, 133, 145, 154, 63, 72, 102, 112, 142, 47, 151, 27, 37, 56, 22, 32, 43, 52, 105, 115, 147,
    160, 65, 169, 74, 156, 9, 19, 61, 70, 165, 178, 83, 187, 24, 34, 92, 174, 125, 135, 46, 55, 107,
    117, 183, 163, 172, 26, 36, 192, 4, 14, 81, 79, 122, 132, 143, 152, 29, 39, 6, 16, 127, 137, 44,
    53, 161, 170, 8, 18, 124, 134, 90, 88, 109, 119, 146, 49, 155, 58, 28, 38, 10, 20, 126, 136, 62,
    64, 104, 114, 149, 179, 181, 158, 71, 73, 106, 116, 144, 48, 153, 57, 129, 30, 139, 40, 80, 82,
    108, 118, 148, 188, 190, 157, 128, 138, 89, 91, 110, 120, 162, 66, 164, 67, 166, 171, 75, 173,
    76, 167, 130, 140, 300, 301, 175, 302, 180, 84, 182, 85, 176, 303, 304, 189, 93, 191, 94, 184,
    305, 185, 306, 193, 307, 194, 308, 309, 310, 311,
)


def kernel(
    p_hbm, r_hbm, cond_ref, gw_ref, pat_ref, live_ref,
    grad_ref, upd_ref,
    rbuf, pall0, pall1, pall2, via, psf, res, mix, part, gath, rows, send, recv, local,
):
    pall = (pall0, pall1, pall2)
    cell = lax.axis_index("cell")
    e = lax.axis_index("elec")
    g = lax.axis_index("gate")
    y, x, zl = cell // (NX * 2), (cell // 2) % NX, cell % 2
    z = e * 2 + zl

    def cell_at(dx, dy, zlow):
        return (((y + dy + NY) % NY) * NX + (x + dx + NX) % NX) * 2 + zlow

    def xy(dx, dy):
        return {"cell": cell_at(dx, dy, zl), "elec": e, "gate": g}

    def at_z(dz, core=None):
        zz = (z + dz + 2 * NZ) % NZ
        return {"cell": cell_at(0, 0, zz % 2), "elec": zz // 2, "gate": g if core is None else core}

    z_mate = at_z(1 - 2 * zl)
    core_mate = {"cell": cell, "elec": e, "gate": 1 - g}
    peers = [at_z(d) for d in (2, 4, 6)]
    cross = [at_z(d, 1 - g) for d in (0, 2, 4, 6)]

    barrier = pltpu.get_barrier_semaphore()
    greet = [xy(1, 0), xy(-1, 0), xy(0, 1), xy(0, -1), at_z(1), at_z(-1)] + peers + cross
    for device in greet:
        pl.semaphore_signal(barrier, inc=1, device_id=device, device_id_type=MESH)

    fetch = pltpu.make_async_copy(r_hbm, res, local.at[3])
    fetch.start()
    own = [
        pltpu.make_async_copy(p_hbm.at[m], pall[m].at[pl.ds(e * 4, 4)], local.at[m])
        for m in range(3)
    ]
    for copy in own:
        copy.start()

    out_row = lax.broadcasted_iota(jnp.int32, (512, 512), 0)
    in_row = lax.broadcasted_iota(jnp.int32, (512, 512), 1)
    shuffle = jnp.where((out_row % 8) * 64 + out_row // 8 == in_row, 1.0, 0.0).astype(jnp.bfloat16)
    fetch.wait()
    turned = jnp.dot(shuffle, res[...], preferred_element_type=jnp.float32)
    rbuf[cell] = turned.astype(jnp.bfloat16).reshape(16, 32, 128)
    for copy in own:
        copy.wait()

    pl.semaphore_wait(barrier, len(greet))

    ids = {}
    copies = {}

    def go(name, src, dst, device):
        n = ids.setdefault(name, len(ids))
        copy = pltpu.make_async_remote_copy(
            src_ref=src, dst_ref=dst, send_sem=send.at[n], recv_sem=recv.at[n],
            device_id=device, device_id_type=MESH,
        )
        copy.start()
        copies[name] = copy

    def residual(name):
        if name == "V0":
            return go(name, rbuf.at[cell], rbuf.at[cell], z_mate)
        s, leg = name[0], name[1]
        second = name[2] == "2" and (leg == "A" or name[3] in "+-")
        sign = 1 if "+" == name[3 if second else 2] else -1
        gone = name[4 if second else 3 :]
        d1 = int(gone) if leg == "B" else 0
        d2 = 0
        if second and leg == "A":
            d1 = sign
        elif second:
            d2 = sign
        along_x = (leg == "A") == (s == "U")
        device = xy(sign, 0) if along_x else xy(0, sign)
        slot = cell_at(-d1, -d2, zl) if s == "U" else cell_at(-d2, -d1, 1 - zl)
        ref = rbuf.at[slot]
        if second:
            ref = rbuf.at[slot, pl.ds(0 if sign == 1 else 8, 8)]
        go(name, ref, ref, device)

    def panel(name):
        kind, m, up = name[:2], int(name[2]), name[3] == "a"
        sign = 1 if up else -1
        first = g * 2 + (0 if up else 1)

        def home(dz):
            return pall[m].at[pl.ds(((z + dz + 2 * NZ) % NZ) // 2 * 4 + first, 1)]

        def stop(n):
            return via.at[n, m, pl.ds(0 if up else 1, 1)]

        mine = home(0)
        if kind == "L1":
            go(name, mine, stop(0), at_z(sign))
        elif kind == "L2":
            go(name, stop(0), home(-sign), at_z(sign))
        elif kind == "L3":
            go(name, home(-2 * sign), stop(1), at_z(sign))
        elif kind == "L4":
            go(name, stop(1), home(-3 * sign), at_z(sign))
        elif kind == "S1":
            go(name, mine, stop(2), at_z(-sign))
        elif kind == "S2":
            go(name, stop(2), home(sign), at_z(-sign))
        else:
            ref = home({"W2": -2, "W4": 4, "WS": 2}[kind] * sign)
            go(name, ref, ref, core_mate)

    def component(m, i, total):
        target = []
        for k in range(4):
            there = pall[m][pat_ref[i, k]]
            alive = jnp.minimum(jnp.maximum(live_ref[i] - k, 0), 1).astype(jnp.float32)
            target.append(there * jnp.full((128, 256), alive).astype(jnp.bfloat16))
        target = jnp.concatenate(target, axis=0)
        for q in range(4):
            left = jnp.concatenate(
                [rbuf[q * 8 : q * 8 + 8, i * 4 + k].reshape(256, 128) for k in range(4)], axis=1
            )
            mix[...] = jnp.dot(left, target, preferred_element_type=jnp.float32)
            for a in range(32):
                row = psf[m, pl.ds(i * 128 + q * 32 + a, 1), :]
                total = total + mix[a * 8 : a * 8 + 8, :] * row
        return total

    total = jnp.zeros((8, 256), jnp.float32)
    for what in PLAN:
        kind, n = what // 100, what % 100
        if kind == 2:
            for m in range(3):
                psf[m] = pall[m][pl.ds(e * 4, 4)].reshape(512, 256).astype(jnp.float32)
        elif kind == 3:
            total = component(n // 4, n % 4, total)
        elif kind == 1:
            copies[NAMES[n]].wait_recv()
        elif NAMES[n][0] in "UV":
            residual(NAMES[n])
        else:
            panel(NAMES[n])

    mine = total * -cond_ref[...]
    weighted = mine[0:1] * gw_ref[0]
    for t in range(1, 8):
        weighted = weighted + mine[t : t + 1] * gw_ref[t]
    part[0:8] = mine
    part[8:16] = jnp.broadcast_to(weighted, (8, 256))
    for n, device in enumerate(peers):
        go(f"G{n}", part, gath.at[e], device)
    for n, device in enumerate(cross):
        go(f"H{n}", part.at[pl.ds(8, 8)], rows.at[e], device)
    gath[e] = part[...]
    for name in copies:
        if name[0] not in "GH":
            copies[name].wait_send()
    for name in copies:
        if name[0] in "GH":
            copies[name].wait_recv()
    grad_ref[...] = (gath[0, 0:8] + gath[1, 0:8]) + (gath[2, 0:8] + gath[3, 0:8])
    here = (gath[0, 8:9] + gath[1, 8:9]) + (gath[2, 8:9] + gath[3, 8:9])
    there = (rows[0, 0:1] + rows[1, 0:1]) + (rows[2, 0:1] + rows[3, 0:1])
    upd_ref[...] = here + there
    for name in copies:
        if name[0] in "GH":
            copies[name].wait_send()


def per_device(panels, conductivity, residuals, gate_weight, pattern, live_count):
    vmem = pl.BlockSpec(memory_space=pltpu.VMEM)
    smem = pl.BlockSpec(memory_space=pltpu.SMEM)
    hbm = pl.BlockSpec(memory_space=pl.ANY)
    copies = 112
    grad, update = pl.pallas_call(
        kernel,
        out_shape=(
            jax.ShapeDtypeStruct((8, 256), jnp.float32),
            jax.ShapeDtypeStruct((1, 256), jnp.float32),
        ),
        in_specs=[hbm, hbm, vmem, smem, smem, smem],
        out_specs=(vmem, vmem),
        scratch_shapes=[
            pltpu.VMEM((32, 16, 32, 128), jnp.bfloat16),
            pltpu.VMEM((16, 128, 256), jnp.bfloat16),
            pltpu.VMEM((16, 128, 256), jnp.bfloat16),
            pltpu.VMEM((16, 128, 256), jnp.bfloat16),
            pltpu.VMEM((3, 3, 2, 128, 256), jnp.bfloat16),
            pltpu.VMEM((3, 512, 256), jnp.float32),
            pltpu.VMEM((512, 128), jnp.bfloat16),
            pltpu.VMEM((256, 256), jnp.float32),
            pltpu.VMEM((16, 256), jnp.float32),
            pltpu.VMEM((4, 16, 256), jnp.float32),
            pltpu.VMEM((4, 8, 256), jnp.float32),
            pltpu.SemaphoreType.DMA((copies,)),
            pltpu.SemaphoreType.DMA((copies,)),
            pltpu.SemaphoreType.DMA((4,)),
        ],
        compiler_params=pltpu.CompilerParams(
            collective_id=0, has_side_effects=True, vmem_limit_bytes=63 << 20
        ),
        name="adjoint",
    )(
        panels.reshape(3, 4, 128, 256),
        residuals.reshape(512, 128),
        conductivity.reshape(1, 256),
        gate_weight,
        pattern,
        live_count,
    )
    return grad, update.reshape(256)


def solution(mesh):
    return jax.shard_map(
        per_device,
        mesh=mesh,
        in_specs=(
            P(None, "elec", "cell"),
            P("cell"),
            P("gate", "elec", None, "cell", None),
            P("gate"),
            P("elec", None),
            P("elec"),
        ),
        out_specs=(P("gate", "cell"), P("cell")),
        check_vma=False,
    )
```

time: 61 us -> 53.5 us (0.88)
  Pallas kernels: 56.3 us -> 50.8 us
  local copies, waits for them, and re-layouts: 3.88 us -> 1.86 us
    pallas_call x1, Pallas kernels: 56.3 us -> 50.8 us  [per_device(): pl.pallas_call(kernel, out_shape=(jax.ShapeDtypeStruct((8, 256), jnp.floa...]
    unnamed x14 -> x4, local copies, waits for them, and re-layouts: 3.88 us -> 1.86 us
where the time goes in v2:
time: 53.5 us; the launch traced here: 53.3 us
  Pallas kernels  50.8 us (95%)
  local copies, waits for them, and re-layouts  1.86 us (3%)
  between operations  0.65 us (1%)
    pallas_call x1, Pallas kernels, per_device(): pl.pallas_call(kernel, out_shape=(jax.ShapeDtypeStruct((8, 256), jnp.floa...  50.8 us
    unnamed x4, local copies, waits for them, and re-layouts  1.86 us

profile of v2, /device:TPU:1, one launch (start us, length us, event | category | flops | bytes accessed | tf_op | source)
XLA Modules:
  0.0 53.3 jit_solution(871131946096896230)
XLA Ops:
  0.6 50.8 %adjoint.1 = (f32[8,256]{1,0:T(8,128)}, f32[1,256]{1,0:T(1,128)}) custom-call(bf16[3,4,128,256]{3,2,1,0:T(8,128)(2,1)} %bitcast.4, bf16[512,128]{1,0:T(8,128)(2,1)} %bitcast.5, f32[1,256]{1,0:T(1,128)} %bitcast.6, f32[8]{0:T(128)} %gw_ref.1, s32[4,4]{1,0:T(4,128)} %pat_ref.1, s32[4]{0:T(128)} %live_ref.1), custom_call_target="tpu_custom_call" | custom-call | tf_op jit(solution)/shard_map/adjoint/pallas_call | solution.py:211
  51.5 0.0 copy-start
  51.5 1.3 %copy.10 = f32[8,256]{1,0:T(8,128)} copy(f32[8,256]{1,0:T(8,128)} %get-tuple-element.8) | data formatting | bytes 16384
  52.8 0.0 copy-done
  52.8 0.6 %copy.11 = f32[256]{0:T(256)} copy(f32[256]{0:T(256)S(1)} %bitcast.7) | data formatting | bytes 2048
Async XLA Ops:
  51.5 1.3 %copy-start = (f32[1,256]{1,0:T(1,128)S(1)}, f32[1,256]{1,0:T(1,128)}, u32[]{:S(2)}) copy-start(f32[1,256]{1,0:T(1,128)} %get-tuple-element.5) | copy-start | bytes 3076

commit v3 on v2

--- a/solution.py
+++ b/solution.py
@@ -27,15 +27,15 @@
     53, 161, 170, 8, 18, 124, 134, 90, 88, 109, 119, 146, 49, 155, 58, 28, 38, 10, 20, 126, 136, 62,
     64, 104, 114, 149, 179, 181, 158, 71, 73, 106, 116, 144, 48, 153, 57, 129, 30, 139, 40, 80, 82,
     108, 118, 148, 188, 190, 157, 128, 138, 89, 91, 110, 120, 162, 66, 164, 67, 166, 171, 75, 173,
-    76, 167, 130, 140, 300, 301, 175, 302, 180, 84, 182, 85, 176, 303, 304, 189, 93, 191, 94, 184,
-    305, 185, 306, 193, 307, 194, 308, 309, 310, 311,
+    76, 167, 130, 140, 300, 301, 302, 175, 303, 180, 84, 182, 85, 176, 304, 305, 306, 307, 184, 189,
+    93, 191, 94, 185, 193, 194, 308, 309, 310, 311,
 )
 
 
 def kernel(
-    p_hbm, r_hbm, cond_ref, gw_ref, pat_ref, live_ref,
+    p_hbm, r_hbm, cond_hbm, gw_hbm, pat_hbm, live_hbm,
     grad_ref, upd_ref,
-    rbuf, pall0, pall1, pall2, via, psf, res, mix, part, gath, rows, send, recv, local,
+    cond_ref, gw_ref, pat_ref, live_ref, rbuf, pall0, pall1, pall2, via, psf, res, mix, part, row, gath, rows, send, recv, local,
 ):
     pall = (pall0, pall1, pall2)
     cell = lax.axis_index("cell")
@@ -69,6 +69,12 @@
     own = [
         pltpu.make_async_copy(p_hbm.at[m], pall[m].at[pl.ds(e * 4, 4)], local.at[m])
         for m in range(3)
+    ]
+    own += [
+        pltpu.make_async_copy(src, dst, local.at[4 + n])
+        for n, (src, dst) in enumerate(
+            ((cond_hbm, cond_ref), (gw_hbm, gw_ref), (pat_hbm, pat_ref), (live_hbm, live_ref))
+        )
     ]
     for copy in own:
         copy.start()
@@ -158,8 +164,8 @@
             )
             mix[...] = jnp.dot(left, target, preferred_element_type=jnp.float32)
             for a in range(32):
-                row = psf[m, pl.ds(i * 128 + q * 32 + a, 1), :]
-                total = total + mix[a * 8 : a * 8 + 8, :] * row
+                source = psf[m, pl.ds(i * 128 + q * 32 + a, 1), :]
+                total = total + mix[a * 8 : a * 8 + 8, :] * source
         return total
 
     total = jnp.zeros((8, 256), jnp.float32)
@@ -181,42 +187,47 @@
     weighted = mine[0:1] * gw_ref[0]
     for t in range(1, 8):
         weighted = weighted + mine[t : t + 1] * gw_ref[t]
-    part[0:8] = mine
-    part[8:16] = jnp.broadcast_to(weighted, (8, 256))
+    part[...] = mine
+    row[...] = weighted
     for n, device in enumerate(peers):
         go(f"G{n}", part, gath.at[e], device)
+    for n, device in enumerate(peers):
+        go(f"H{n}", row, rows.at[g, e], device)
     for n, device in enumerate(cross):
-        go(f"H{n}", part.at[pl.ds(8, 8)], rows.at[e], device)
-    gath[e] = part[...]
+        go(f"I{n}", row, rows.at[g, e], device)
+    gath[e] = mine
+    rows[g, e] = weighted
     for name in copies:
-        if name[0] not in "GH":
+        if name[0] not in "GHI":
             copies[name].wait_send()
     for name in copies:
-        if name[0] in "GH":
+        if name[0] in "GHI":
             copies[name].wait_recv()
-    grad_ref[...] = (gath[0, 0:8] + gath[1, 0:8]) + (gath[2, 0:8] + gath[3, 0:8])
-    here = (gath[0, 8:9] + gath[1, 8:9]) + (gath[2, 8:9] + gath[3, 8:9])
-    there = (rows[0, 0:1] + rows[1, 0:1]) + (rows[2, 0:1] + rows[3, 0:1])
-    upd_ref[...] = here + there
+    grad_ref[...] = (gath[0] + gath[1]) + (gath[2] + gath[3])
+    each = [(rows[n, 0] + rows[n, 1]) + (rows[n, 2] + rows[n, 3]) for n in range(2)]
+    upd_ref[...] = each[0] + each[1]
     for name in copies:
-        if name[0] in "GH":
+        if name[0] in "GHI":
             copies[name].wait_send()
 
 
 def per_device(panels, conductivity, residuals, gate_weight, pattern, live_count):
     vmem = pl.BlockSpec(memory_space=pltpu.VMEM)
-    smem = pl.BlockSpec(memory_space=pltpu.SMEM)
     hbm = pl.BlockSpec(memory_space=pl.ANY)
     copies = 112
     grad, update = pl.pallas_call(
         kernel,
         out_shape=(
-            jax.ShapeDtypeStruct((8, 256), jnp.float32),
-            jax.ShapeDtypeStruct((1, 256), jnp.float32),
+            pltpu.VMEM((8, 256), jnp.float32),
+            pltpu.VMEM((1, 256), jnp.float32),
         ),
-        in_specs=[hbm, hbm, vmem, smem, smem, smem],
+        in_specs=[hbm] * 6,
         out_specs=(vmem, vmem),
         scratch_shapes=[
+            pltpu.VMEM((1, 256), jnp.float32),
+            pltpu.SMEM((8,), jnp.float32),
+            pltpu.SMEM((4, 4), jnp.int32),
+            pltpu.SMEM((4,), jnp.int32),
             pltpu.VMEM((32, 16, 32, 128), jnp.bfloat16),
             pltpu.VMEM((16, 128, 256), jnp.bfloat16),
             pltpu.VMEM((16, 128, 256), jnp.bfloat16),
@@ -225,15 +236,16 @@
             pltpu.VMEM((3, 512, 256), jnp.float32),
             pltpu.VMEM((512, 128), jnp.bfloat16),
             pltpu.VMEM((256, 256), jnp.float32),
-            pltpu.VMEM((16, 256), jnp.float32),
-            pltpu.VMEM((4, 16, 256), jnp.float32),
+            pltpu.VMEM((8, 256), jnp.float32),
+            pltpu.VMEM((1, 256), jnp.float32),
             pltpu.VMEM((4, 8, 256), jnp.float32),
+            pltpu.VMEM((2, 4, 1, 256), jnp.float32),
             pltpu.SemaphoreType.DMA((copies,)),
             pltpu.SemaphoreType.DMA((copies,)),
-            pltpu.SemaphoreType.DMA((4,)),
+            pltpu.SemaphoreType.DMA((8,)),
         ],
         compiler_params=pltpu.CompilerParams(
-            collective_id=0, has_side_effects=True, vmem_limit_bytes=63 << 20
+            collective_id=0, has_side_effects=True, vmem_limit_bytes=60 << 20
         ),
         name="adjoint",
     )(

time: 53.5 us -> 51.1 us (0.955)
  Pallas kernels: 50.8 us -> 49.2 us
  local copies, waits for them, and re-layouts: 1.86 us -> 1.16 us
    pallas_call x1, Pallas kernels: 50.8 us -> 49.2 us  [per_device(): pl.pallas_call(kernel, out_shape=(pltpu.VMEM((8, 256), jnp.float32), pltp...]
    unnamed x4 -> x2, local copies, waits for them, and re-layouts: 1.86 us -> 1.16 us
where the time goes in v3:
time: 51.1 us; the launch traced here: 51 us
  Pallas kernels  49.2 us (96%)
  local copies, waits for them, and re-layouts  1.16 us (2%)
  between operations  0.64 us (1%)
    pallas_call x1, Pallas kernels, per_device(): pl.pallas_call(kernel, out_shape=(pltpu.VMEM((8, 256), jnp.float32), pltp...  49.2 us
    unnamed x2, local copies, waits for them, and re-layouts  1.16 us

profile of v3, /device:TPU:1, one launch (start us, length us, event | category | flops | bytes accessed | tf_op | source)
XLA Modules:
  0.0 51.0 jit_solution(1464796127247476523)
XLA Ops:
  0.6 49.2 %adjoint.1 = (f32[8,256]{1,0:T(8,128)S(1)}, f32[1,256]{1,0:T(1,128)S(1)}) custom-call(bf16[3,4,128,256]{3,2,1,0:T(8,128)(2,1)} %bitcast.5, bf16[512,128]{1,0:T(8,128)(2,1)} %bitcast.6, f32[1,256]{1,0:T(1,128)} %bitcast.7, f32[8]{0:T(128)} %gw_hbm.1, s32[4,4]{1,0:T(4,128)} %pat_hbm.1, s32[4]{0:T(128)} %live_hbm.1), custom_call_target="tpu_custom_call" | custom-call | tf_op jit(solution)/shard_map/adjoint/pallas_call | solution.py:218
  49.8 0.6 %copy.10 = f32[8,256]{1,0:T(8,128)} copy(f32[8,256]{1,0:T(8,128)S(1)} %get-tuple-element.6) | data formatting | bytes 16384
  50.4 0.6 %copy.11 = f32[256]{0:T(256)} copy(f32[256]{0:T(256)S(1)} %bitcast.4) | data formatting | bytes 2048

commit v4 on v3

--- a/solution.py
+++ b/solution.py
@@ -11,24 +11,26 @@
 NAMES = ["V0"]
 for s in "UV":
     for way in "+-":
-        NAMES += [s + "A" + way, s + "A2" + way]
+        NAMES += [s + "A" + way, s + "C" + way, s + "A2" + way]
         for gone in (0, 1, -1, 2):
-            NAMES += [s + "B" + way + str(gone), s + "B2" + way + str(gone)]
+            NAMES += [s + kind + way + str(gone) for kind in ("B", "D", "B2")]
 for m in "012":
     for way in "ab":
         NAMES += [kind + m + way for kind in ("L1", "L2", "L3", "L4", "S1", "S2", "W2", "W4", "WS")]
 
 PLAN = (
-    0, 1, 11, 3, 13, 41, 50, 59, 68, 200, 77, 86, 100, 21, 31, 23, 33, 45, 54, 141, 150, 101, 111,
-    103, 113, 5, 15, 2, 12, 42, 51, 159, 168, 60, 69, 177, 186, 7, 17, 78, 87, 121, 25, 35, 131,
-    123, 133, 145, 154, 63, 72, 102, 112, 142, 47, 151, 27, 37, 56, 22, 32, 43, 52, 105, 115, 147,
-    160, 65, 169, 74, 156, 9, 19, 61, 70, 165, 178, 83, 187, 24, 34, 92, 174, 125, 135, 46, 55, 107,
-    117, 183, 163, 172, 26, 36, 192, 4, 14, 81, 79, 122, 132, 143, 152, 29, 39, 6, 16, 127, 137, 44,
-    53, 161, 170, 8, 18, 124, 134, 90, 88, 109, 119, 146, 49, 155, 58, 28, 38, 10, 20, 126, 136, 62,
-    64, 104, 114, 149, 179, 181, 158, 71, 73, 106, 116, 144, 48, 153, 57, 129, 30, 139, 40, 80, 82,
-    108, 118, 148, 188, 190, 157, 128, 138, 89, 91, 110, 120, 162, 66, 164, 67, 166, 171, 75, 173,
-    76, 167, 130, 140, 300, 301, 302, 175, 303, 180, 84, 182, 85, 176, 304, 305, 306, 307, 184, 189,
-    93, 191, 94, 185, 193, 194, 308, 309, 310, 311,
+    0, 1, 17, 4, 20, 61, 70, 2, 16, 5, 19, 400, 79, 88, 97, 106, 200, 31, 47, 34, 50, 201, 217, 204,
+    220, 32, 46, 3, 18, 65, 74, 261, 270, 202, 216, 205, 219, 7, 23, 35, 49, 62, 71, 279, 288, 10,
+    26, 80, 89, 231, 37, 52, 247, 234, 250, 297, 306, 33, 48, 41, 56, 98, 107, 232, 246, 203, 218,
+    265, 274, 13, 29, 40, 53, 83, 92, 207, 223, 235, 249, 262, 67, 271, 76, 8, 22, 38, 55, 63, 72,
+    210, 226, 237, 252, 267, 280, 85, 289, 94, 276, 11, 25, 36, 51, 81, 90, 233, 248, 241, 256, 285,
+    298, 103, 307, 112, 294, 14, 28, 43, 59, 66, 75, 213, 229, 240, 253, 303, 283, 292, 312, 6, 21,
+    44, 58, 101, 99, 208, 222, 238, 255, 263, 272, 9, 24, 39, 54, 64, 73, 211, 225, 236, 251, 281,
+    290, 12, 27, 42, 57, 110, 108, 214, 228, 243, 259, 266, 69, 275, 78, 15, 30, 45, 60, 82, 84,
+    206, 221, 244, 258, 269, 299, 301, 278, 91, 93, 209, 224, 239, 254, 264, 68, 273, 77, 100, 102,
+    212, 227, 242, 257, 268, 308, 310, 277, 109, 111, 215, 230, 245, 260, 600, 282, 86, 284, 87,
+    601, 602, 603, 286, 291, 95, 293, 96, 287, 295, 300, 104, 302, 105, 296, 604, 605, 606, 607,
+    304, 309, 113, 311, 114, 305, 313, 314, 608, 609, 610, 611,
 )
 
 
@@ -56,11 +58,11 @@
 
     z_mate = at_z(1 - 2 * zl)
     core_mate = {"cell": cell, "elec": e, "gate": 1 - g}
-    peers = [at_z(d) for d in (2, 4, 6)]
-    cross = [at_z(d, 1 - g) for d in (0, 2, 4, 6)]
+    peers = [at_z(d) for d in (4, 2, 6)]
+    cross = [at_z(d, 1 - g) for d in (4, 2, 6, 0)]
 
     barrier = pltpu.get_barrier_semaphore()
-    greet = [xy(1, 0), xy(-1, 0), xy(0, 1), xy(0, -1), at_z(1), at_z(-1)] + peers + cross
+    greet = [xy(1, 0), xy(-1, 0), xy(0, 1), xy(0, -1), at_z(1), at_z(-1), core_mate]
     for device in greet:
         pl.semaphore_signal(barrier, inc=1, device_id=device, device_id_type=MESH)
 
@@ -106,21 +108,16 @@
         if name == "V0":
             return go(name, rbuf.at[cell], rbuf.at[cell], z_mate)
         s, leg = name[0], name[1]
-        second = name[2] == "2" and (leg == "A" or name[3] in "+-")
-        sign = 1 if "+" == name[3 if second else 2] else -1
+        second = name[2] == "2"
+        sign = 1 if name[3 if second else 2] == "+" else -1
         gone = name[4 if second else 3 :]
-        d1 = int(gone) if leg == "B" else 0
-        d2 = 0
-        if second and leg == "A":
-            d1 = sign
-        elif second:
-            d2 = sign
-        along_x = (leg == "A") == (s == "U")
-        device = xy(sign, 0) if along_x else xy(0, sign)
+        first_axis = leg in "AC"
+        half = (0 if sign == 1 else 1) if second else (0 if leg in "AB" else 1)
+        d1 = (sign if second else 0) if first_axis else int(gone)
+        d2 = sign if second and not first_axis else 0
+        device = xy(sign, 0) if first_axis == (s == "U") else xy(0, sign)
         slot = cell_at(-d1, -d2, zl) if s == "U" else cell_at(-d2, -d1, 1 - zl)
-        ref = rbuf.at[slot]
-        if second:
-            ref = rbuf.at[slot, pl.ds(0 if sign == 1 else 8, 8)]
+        ref = rbuf.at[slot, pl.ds(half * 8, 8)]
         go(name, ref, ref, device)
 
     def panel(name):
@@ -170,7 +167,7 @@
 
     total = jnp.zeros((8, 256), jnp.float32)
     for what in PLAN:
-        kind, n = what // 100, what % 100
+        kind, n = what // 200, what % 200
         if kind == 2:
             for m in range(3):
                 psf[m] = pall[m][pl.ds(e * 4, 4)].reshape(512, 256).astype(jnp.float32)
@@ -214,7 +211,7 @@
 def per_device(panels, conductivity, residuals, gate_weight, pattern, live_count):
     vmem = pl.BlockSpec(memory_space=pltpu.VMEM)
     hbm = pl.BlockSpec(memory_space=pl.ANY)
-    copies = 112
+    copies = 128
     grad, update = pl.pallas_call(
         kernel,
         out_shape=(

time: 51.1 us -> 49.8 us (0.975)
  Pallas kernels: 49.2 us -> 47.9 us
    pallas_call x1, Pallas kernels: 49.2 us -> 47.9 us  [per_device(): pl.pallas_call(kernel, out_shape=(pltpu.VMEM((8, 256), jnp.float32), pltp...]
where the time goes in v4:
time: 49.8 us; the launch traced here: 49.7 us
  Pallas kernels  47.9 us (96%)
  local copies, waits for them, and re-layouts  1.16 us (2%)
  between operations  0.64 us (1%)
    pallas_call x1, Pallas kernels, per_device(): pl.pallas_call(kernel, out_shape=(pltpu.VMEM((8, 256), jnp.float32), pltp...  47.9 us
    unnamed x2, local copies, waits for them, and re-layouts  1.16 us

profile of v4, /device:TPU:1, one launch (start us, length us, event | category | flops | bytes accessed | tf_op | source)
XLA Modules:
  0.0 49.7 jit_solution(486963439409213181)
XLA Ops:
  0.6 47.9 %adjoint.1 = (f32[8,256]{1,0:T(8,128)S(1)}, f32[1,256]{1,0:T(1,128)S(1)}) custom-call(bf16[3,4,128,256]{3,2,1,0:T(8,128)(2,1)} %bitcast.5, bf16[512,128]{1,0:T(8,128)(2,1)} %bitcast.6, f32[1,256]{1,0:T(1,128)} %bitcast.7, f32[8]{0:T(128)} %gw_hbm.1, s32[4,4]{1,0:T(4,128)} %pat_hbm.1, s32[4]{0:T(128)} %live_hbm.1), custom_call_target="tpu_custom_call" | custom-call | tf_op jit(solution)/shard_map/adjoint/pallas_call | solution.py:215
  48.6 0.6 %copy.10 = f32[8,256]{1,0:T(8,128)} copy(f32[8,256]{1,0:T(8,128)S(1)} %get-tuple-element.6) | data formatting | bytes 16384
  49.2 0.6 %copy.11 = f32[256]{0:T(256)} copy(f32[256]{0:T(256)S(1)} %bitcast.4) | data formatting | bytes 2048

commit v5 on v4

--- a/solution.py
+++ b/solution.py
@@ -28,8 +28,8 @@
     44, 58, 101, 99, 208, 222, 238, 255, 263, 272, 9, 24, 39, 54, 64, 73, 211, 225, 236, 251, 281,
     290, 12, 27, 42, 57, 110, 108, 214, 228, 243, 259, 266, 69, 275, 78, 15, 30, 45, 60, 82, 84,
     206, 221, 244, 258, 269, 299, 301, 278, 91, 93, 209, 224, 239, 254, 264, 68, 273, 77, 100, 102,
-    212, 227, 242, 257, 268, 308, 310, 277, 109, 111, 215, 230, 245, 260, 600, 282, 86, 284, 87,
-    601, 602, 603, 286, 291, 95, 293, 96, 287, 295, 300, 104, 302, 105, 296, 604, 605, 606, 607,
+    212, 227, 242, 257, 268, 308, 310, 277, 109, 111, 215, 230, 245, 260, 282, 86, 284, 87, 600,
+    601, 602, 603, 286, 291, 95, 293, 96, 287, 300, 104, 302, 105, 295, 296, 604, 605, 606, 607,
     304, 309, 113, 311, 114, 305, 313, 314, 608, 609, 610, 611,
 )
 
@@ -87,9 +87,6 @@
     fetch.wait()
     turned = jnp.dot(shuffle, res[...], preferred_element_type=jnp.float32)
     rbuf[cell] = turned.astype(jnp.bfloat16).reshape(16, 32, 128)
-    for copy in own:
-        copy.wait()
-
     pl.semaphore_wait(barrier, len(greet))
 
     ids = {}
@@ -131,7 +128,7 @@
         def stop(n):
             return via.at[n, m, pl.ds(0 if up else 1, 1)]
 
-        mine = home(0)
+        mine = p_hbm.at[m, pl.ds(first, 1)]
         if kind == "L1":
             go(name, mine, stop(0), at_z(sign))
         elif kind == "L2":
@@ -169,6 +166,8 @@
     for what in PLAN:
         kind, n = what // 200, what % 200
         if kind == 2:
+            for copy in own:
+                copy.wait()
             for m in range(3):
                 psf[m] = pall[m][pl.ds(e * 4, 4)].reshape(512, 256).astype(jnp.float32)
         elif kind == 3:

time: 49.8 us -> 49.6 us (level)
  no operation moved by 1% of the time
where the time goes in v5:
time: 49.6 us; the launch traced here: 49.5 us
  Pallas kernels  47.7 us (96%)
  local copies, waits for them, and re-layouts  1.16 us (2%)
  between operations  0.64 us (1%)
    pallas_call x1, Pallas kernels, per_device(): pl.pallas_call(kernel, out_shape=(pltpu.VMEM((8, 256), jnp.float32), pltp...  47.7 us
    unnamed x2, local copies, waits for them, and re-layouts  1.16 us

profile of v5, /device:TPU:1, one launch (start us, length us, event | category | flops | bytes accessed | tf_op | source)
XLA Modules:
  0.0 49.5 jit_solution(12052264935539847385)
XLA Ops:
  0.6 47.7 %adjoint.1 = (f32[8,256]{1,0:T(8,128)S(1)}, f32[1,256]{1,0:T(1,128)S(1)}) custom-call(bf16[3,4,128,256]{3,2,1,0:T(8,128)(2,1)} %bitcast.5, bf16[512,128]{1,0:T(8,128)(2,1)} %bitcast.6, f32[1,256]{1,0:T(1,128)} %bitcast.7, f32[8]{0:T(128)} %gw_hbm.1, s32[4,4]{1,0:T(4,128)} %pat_hbm.1, s32[4]{0:T(128)} %live_hbm.1), custom_call_target="tpu_custom_call" | custom-call | tf_op jit(solution)/shard_map/adjoint/pallas_call | solution.py:214
  48.3 0.6 %copy.10 = f32[8,256]{1,0:T(8,128)} copy(f32[8,256]{1,0:T(8,128)S(1)} %get-tuple-element.6) | data formatting | bytes 16384
  48.9 0.6 %copy.11 = f32[256]{0:T(256)} copy(f32[256]{0:T(256)S(1)} %bitcast.4) | data formatting | bytes 2048
